TPU v7x, 128 devices: a whole 4x4x4 slice. The times are simulated.
128 devices in a mesh: grp: 4 (over y_hi, core), row: 8 (over y_lo, z), col: 4 (over x).
Axes of the slice: x: 4, y: 4 (y_hi: 2, y_lo: 2; y = y_hi * 2 + y_lo), z: 4, core: 2. Of those that a mesh axis runs over, the one named last changes fastest.
Arguments:
- density: bfloat16 [1024, 15, 128, 128], P(('grp', 'row', 'col')), may hold values from -0.29882812 to 0.29882812
- block_mask: int32 [1024, 15], P(('grp', 'row', 'col')), may hold values 0 or 1
- orbital_cell: int32 [131072], P(('grp', 'row', 'col')), may hold values from 0 to 16383
- slab_of_device: int32 [128], replicated, may hold values from 0 to 127, each once
- positions: float32 [3, 65536], P(None, ('grp', 'row', 'col')), may hold values from 0 to 1
- charges: float32 [65536], P(('grp', 'row', 'col')), may hold values from -3 to 3
Outputs:
- new_density: bfloat16 [1024, 15, 128, 128], P(('grp', 'row', 'col'))
- energies: float32 [65536], P(('grp', 'row', 'col'))
Inputs may be any that keep to these rules, and one draw needn't show every extreme that they name: `orbital_cell`: cell numbers lie within one slab of 1 planes. `slab_of_device`: a permutation of the slabs.
All inputs are finite; a program needn't handle non-finite values. No bound on the sum of `block_mask` on one device may be relied on, other than what follows from the above.
Results may differ from a plain program's by a relative error of at most 0.0031.
Values may be sent and summed in bfloat16 or wider, within the bound.
A program may use at most 128 MiB of HBM per device.

v0:
```python
import jax
import jax.numpy as jnp
from jax import lax
from jax.sharding import PartitionSpec as P

BS = 128
BAND = 7
SLOTS = 15
PLANES_DEV = 1
GRID_Y = 128
GRID_Z = 128


SPREAD = 2.0
COUPLE = 0.5
DENSITY_SCALE = 0.05


def with_halo(block, sides, width):
    for axis, dim in sides:
        count = lax.axis_size(axis)
        forward = [(i, i + 1) for i in range(count - 1)]
        backward = [(target, source) for source, target in forward]
        low = lax.ppermute(
            lax.slice_in_dim(block, block.shape[dim] - width, None, axis=dim), axis, forward
        )
        high = lax.ppermute(lax.slice_in_dim(block, 0, width, axis=dim), axis, backward)
        block = jnp.concatenate([low, block, high], axis=dim)
    return block


def gaussian(centre, points):
    offset = points[:, None] - centre[None, :]
    return jnp.exp(-offset * offset / (2.0 * SPREAD * SPREAD))


def atom_tables(positions, grid_x):
    height = jnp.arange(GRID_Y, dtype=jnp.float32)
    depth = jnp.arange(GRID_Z, dtype=jnp.float32)
    return (
        positions[0] * grid_x,
        gaussian(positions[1] * GRID_Y, height),
        gaussian(positions[2] * GRID_Z, depth),
    )


def plane_potential(plane_id, xcoord, along_y, along_z, charges):
    weight = gaussian(xcoord, plane_id.astype(jnp.float32)[None])[0] * charges
    return jnp.dot(along_y * weight[None, :], along_z.T, precision=lax.Precision.HIGHEST)


def plane_energy(rho_plane, plane_id, xcoord, along_y, along_z):
    weight = gaussian(xcoord, plane_id.astype(jnp.float32)[None])[0]
    inner_sum = jnp.dot(rho_plane, along_z, precision=lax.Precision.HIGHEST)
    return weight * jnp.sum(inner_sum * along_y, axis=0)


def make_work(density, valid_blocks, shifts):
    masked = density * valid_blocks.astype(jnp.bfloat16)[:, :, None, None]
    identity = jnp.eye(BS, dtype=jnp.float32)
    centre_block = (
        density[:, BAND].astype(jnp.float32) - shifts[:, :, None] * identity[None]
    ) * valid_blocks[:, BAND][:, None, None]
    return masked.at[:, BAND].set(centre_block.astype(jnp.bfloat16))


def band_square(padded, number):
    results = []
    for slot in range(SLOTS):
        lowest = max(0, slot - BAND)
        highest = min(SLOTS - 1, slot + BAND)
        left_side = padded[BAND : BAND + number, lowest : highest + 1]
        right_side = jnp.stack(
            [
                padded[shift_id : shift_id + number, slot - shift_id + BAND]
                for shift_id in range(lowest, highest + 1)
            ],
            axis=1,
        )
        results.append(
            jnp.einsum("raij,rajk->rik", left_side, right_side, preferred_element_type=jnp.float32)
        )
    return jnp.stack(results, axis=1)


def on_device(density, block_mask, orbital_cell, slab_of_device, positions, charges):
    members = lax.axis_size(("grp", "row", "col"))
    my_index = lax.axis_index(("grp", "row", "col"))
    grid_x = PLANES_DEV * members
    nrows_here = density.shape[0]
    atoms_here = charges.shape[0]
    xcoord, along_y, along_z = atom_tables(positions, grid_x)

    def whole_plane(row_id):
        return slab_of_device[row_id // PLANES_DEV] * PLANES_DEV + row_id % PLANES_DEV

    row_ids = jnp.arange(lax.axis_size(("grp", "row", "col")) * PLANES_DEV, dtype=jnp.int32)
    potential = lax.psum_scatter(
        lax.map(
            lambda row_id: plane_potential(whole_plane(row_id), xcoord, along_y, along_z, charges),
            row_ids,
        ),
        ("grp", "row", "col"),
        scatter_dimension=0,
        tiled=True,
    )
    shifts = (COUPLE * potential.reshape(-1)[orbital_cell]).reshape(nrows_here, BS)
    global_rows = my_index * nrows_here + jnp.arange(nrows_here, dtype=jnp.int32)
    columns = global_rows[:, None] + jnp.arange(SLOTS, dtype=jnp.int32)[None, :] - BAND
    inside = ((columns >= 0) & (columns < nrows_here * members)).astype(jnp.int32)
    valid_blocks = (block_mask * inside).astype(jnp.float32)
    work = make_work(density, valid_blocks, shifts)
    padded = with_halo(work, ((("grp", "row", "col"), 0),), BAND)
    squared = band_square(padded, nrows_here)
    own_rows = padded[BAND : BAND + nrows_here].astype(jnp.float32)
    new_density = (valid_blocks[:, :, None, None] * (2.0 * own_rows - squared)).astype(jnp.bfloat16)
    diagonal_values = (
        jnp.diagonal(new_density[:, BAND], axis1=1, axis2=2).astype(jnp.float32).reshape(-1)
        * DENSITY_SCALE
    )
    cells_here = PLANES_DEV * GRID_Y * GRID_Z
    grid_density = jnp.zeros((cells_here,), jnp.float32).at[orbital_cell].add(diagonal_values)
    grid_density = grid_density.reshape(PLANES_DEV, GRID_Y, GRID_Z)
    piece = lax.all_gather(
        grid_density.astype(jnp.bfloat16), ("grp", "row", "col"), axis=0, tiled=True
    ).astype(jnp.float32)

    def one_row(step_id, accum):
        return accum + plane_energy(piece[step_id], whole_plane(step_id), xcoord, along_y, along_z)

    gathered = lax.fori_loop(0, piece.shape[0], one_row, jnp.zeros((atoms_here,), jnp.float32))
    energies = charges * gathered
    return (new_density, energies)


def solution(mesh):
    in_specs = (
        P(("grp", "row", "col"), None, None, None),
        P(("grp", "row", "col"), None),
        P(("grp", "row", "col")),
        P(),
        P(None, ("grp", "row", "col")),
        P(("grp", "row", "col")),
    )
    out_specs = (P(("grp", "row", "col"), None, None, None), P(("grp", "row", "col")))
    return jax.shard_map(
        on_device, mesh=mesh, in_specs=in_specs, out_specs=out_specs, check_vma=False
    )
```

profile of v0, /device:TPU:1, one launch (start us, length us, event | category | flops | bytes accessed | tf_op | source)
XLA Modules:
  0.0 2223.4 jit_solution(8334465923963774730)
XLA Ops:
  8.0 794.9 %while.32 = (s32[]{:T(128)}, f32[128,128,128]{2,1,0:T(8,128)}, s32[128]{0:T(128)S(1)}, s32[128]{0:T(128)}, f32[512]{0:T(512)S(1)}, /*index=5*/f32[512]{0:T(512)}...) while((s32[]{:T(128)}, f32[128,128,128]{2,1,0:T(8,128)}, ...), condition=%wide.region_1.2_spmd.clone, body=%wide.region_0.1_spmd.clone.sunk | while | flops 101255688 | bytes 78515 | solution.py:99
  804.0 4.4 broadcast_multiply_fusion
  808.3 599.9 %reduce-scatter.2.cloned.1.call-done = f32[1,128,128]{2,1,0:T(8,128)} async-done(((f32[128,128,128]{2,1,0:T(8,128)}), f32[1,128,128]{2,1,0:T(8,128)}) %reduce-scatter.2.cloned.1.call-update) | async-done | bytes 65552 | tf_op jit(solution)/shard_map/reduce_scatter | solution.py:98
  1408.3 5.9 gather_fusion
  1414.2 1.9 constant_dynamic-update-slice_fusion.169
  1416.0 4.7 fusion.220
  1420.7 1.9 collective-permute-start
  1422.6 8.0 collective-permute-start.1
  1430.7 72.8 %collective-permute-done = bf16[7,15,128,128]{3,2,1,0:T(8,128)(2,1)S(1)} collective-permute-done((bf16[7,15,128,128]{3,2,1,0:T(8,128)(2,1)S(1)}, bf16[7,15,128,128]{3,2,1,0:T(8,128)(2,1)S(1)}, u32[]{:S(2)}, u32[]{:S(2)}) %collective-permute-start) | collective-permute-done | bytes 3440672 | tf_op jit(solution)/shard_map/ppermute | solution.py:24
  1503.5 1.4 constant_dynamic-update-slice_fusion.160
  1505.0 1.3 constant_dynamic-update-slice_fusion.151
  1506.3 1.3 constant_dynamic-update-slice_fusion.140
  1523.3 2.3 constant_dynamic-update-slice_fusion.155
  1525.7 1.3 copy-done.6
  1527.0 2.5 fusion.47
  1529.5 1.4 constant_dynamic-update-slice_fusion.154
  1533.0 2.4 fusion.59
  1538.8 1.8 copy-done.4
  1540.8 1.3 constant_dynamic-update-slice_fusion.142
  1544.4 2.9 fusion.56
  1559.1 3.9 multiply_convert_fusion
  1564.0 3.1 copy.11
  1567.1 1.9 gather_fusion.1
  1569.1 6.0 scatter_custom_fusion
  1575.8 320.0 %all-gather.2.cloned.1.call-done = bf16[128,128,128]{2,1,0:T(8,128)(2,1)} async-done(((bf16[1,128,128]{2,1,0:T(8,128)(2,1)}), bf16[128,128,128]{2,1,0:T(8,128)(2,1)}) %all-gather.2.cloned.1.call-update) | async-done | bytes 4194320 | tf_op jit(solution)/shard_map/all_gather | solution.py:124
  1895.8 6.5 convert_element_type.84
  1902.3 313.7 %while.33 = (s32[]{:T(128)}, f32[512]{0:T(512)S(1)}, s32[128]{0:T(128)S(1)}, f32[512]{0:T(512)S(1)}, f32[128,128,128]{2,1,0:T(8,128)}, /*index=5*/f32[512]{0:T(512)S(1)}, f32[512]{0:T(512)S(1)}, s32[]{:T(128)}, s32[]{:T(128)}) while((s32[]{:T(128)}, f32[512]{0:T(512)S(1)}, s32[128]{0:T(128)S(1)}, f32[512]{0:T(512)S(1)}, ...), condition=%wide.region_6.7_spmd.clone, body=%wide.region_4.6_spmd.clone.sunk | while | flops 101321728 | bytes 80511 | solution.py:131
  1902.3 1.3 fusion.265
  1904.8 1.3 fusion.265
  1909.7 1.3 fusion.265
  1917.1 1.3 fusion.265
  1924.4 1.3 fusion.265
  1929.3 1.3 fusion.265
  1931.8 1.3 fusion.265
  1936.7 1.3 fusion.265
  1939.1 1.3 fusion.265
  1944.0 1.3 fusion.265
  1946.5 1.3 fusion.265
  1951.4 1.3 fusion.265
  1953.8 1.3 fusion.265
  1958.7 1.3 fusion.265
  1961.2 1.3 fusion.265
  1966.1 1.3 fusion.265
  1973.4 1.3 fusion.265
  1980.8 1.3 fusion.265
  1988.1 1.3 fusion.265
  1995.5 1.3 fusion.265
  2002.8 1.3 fusion.265
  (962 shorter events, 714.6 us)
Async XLA Ops:
  7.2 1401.1 %reduce-scatter.2.cloned.1.call-start = ((), (), s32[]{:S(2)}) async-start(), calls=%async_computation.1 | async-start | bytes 8454144 | tf_op jit(solution)/shard_map/reduce_scatter | solution.py:98
  803.0 0.7 copy-start.10
  803.0 1.0 copy-start.9
  803.0 1092.8 %all-gather.2.cloned.1.call-start = ((), (), s32[]{:S(2)}) async-start(), calls=%async_computation.2 | async-start | bytes 4227072 | tf_op jit(solution)/shard_map/all_gather | solution.py:124
  1416.0 87.5 %copy-start = (bf16[8,15,128,128]{3,2,1,0:T(8,128)(2,1)S(1)}, bf16[8,15,128,128]{3,2,1,0:T(8,128)(2,1)}, u32[]{:S(2)}) copy-start(bf16[8,15,128,128]{3,2,1,0:T(8,128)(2,1)} %constant_dynamic-update-slice_fusion.169) | copy-start | bytes 11796484
  1420.7 82.8 %collective-permute-start = (bf16[7,15,128,128]{3,2,1,0:T(8,128)(2,1)S(1)}, bf16[7,15,128,128]{3,2,1,0:T(8,128)(2,1)S(1)}, u32[]{:S(2)}, u32[]{:S(2)}) collective-permute-start(bf16[7,15,128,128]{3,2,1,0:T(8,128)(2,1)S(1)} %get-tuple-element.590), channel_id=1, source_target_pairs={{0,1},{1,2},{2,3},{3,4},{4,5},{5,6},{6,7},{7,8},{8,9},{9,10},{10,1... | collective-permute-start | bytes 10321928 | tf_op jit(solution)/shard_map/ppermute | solution.py:24
  1422.6 85.0 %collective-permute-start.1 = (bf16[7,15,128,128]{3,2,1,0:T(8,128)(2,1)S(1)}, bf16[7,15,128,128]{3,2,1,0:T(8,128)(2,1)S(1)}, u32[]{:S(2)}, u32[]{:S(2)}) collective-permute-start(bf16[7,15,128,128]{3,2,1,0:T(8,128)(2,1)S(1)} %get-tuple-element.589), channel_id=1, source_target_pairs={{1,0},{2,1},{3,2},{4,3},{5,4},{6,5},{7,6},{8,7},{9,8},{10,9},{11,1... | collective-permute-start | bytes 10321928 | tf_op jit(solution)/shard_map/ppermute | solution.py:27
  1507.6 1.9 copy-start.3
  1523.3 2.3 copy-start.2
  1525.7 1.3 copy-start.6
  1527.0 2.5 copy-start.1
  1538.7 1.8 copy-start.4
  1555.5 1.7 copy-start.5
  1556.3 1.8 copy-start.7
  1575.8 326.6 %copy-start.11 = (s32[128]{0:T(128)S(1)}, s32[128]{0:T(128)}, u32[]{:S(2)}) copy-start(s32[128]{0:T(128)} %get-tuple-element.765) | copy-start | bytes 1540
  1902.3 313.7 %copy-start.8 = (f32[512]{0:T(512)S(1)}, f32[512]{0:T(512)}, u32[]{:S(2)}) copy-start(f32[512]{0:T(512)} %get-tuple-element.762) | copy-start | bytes 6148
Sparse Core Ops, SparseCore 0:
  803.1 605.0 reduce-scatter.1
  1575.9 319.8 all-gather.1
where the time goes:
time: 2240 us; the launch traced here: 2220 us
  waiting for transfers between devices  993 us (44%)
  loops' own time  406 us (18%)
  local copies, waits for them, and re-layouts  328 us (15%)
  matrix products  326 us (15%)
  other arithmetic  147 us (7%)
    reduce_scatter x1, waiting for transfers between devices, on_device(): lax.psum_scatter(lax.map(lambda row_id: plane_potential(whole_plane(row_i...  600 us
    another operation x1, loops' own time, on_device(): lax.map(lambda row_id: plane_potential(whole_plane(row_id), xcoord, along...  332 us
    all_gather x1, waiting for transfers between devices, on_device(): lax.all_gather(grid_density.astype(jnp.bfloat16), ('grp', 'row', 'col'),...  320 us
    dynamic_slice x256, local copies, waits for them, and re-layouts, whole_plane(): slab_of_device[row_id // PLANES_DEV] * PLANES_DEV + row_id % PLANES_DEV  230 us
    dot_general x128, matrix products, plane_energy(): inner_sum = jnp.dot(rho_plane, along_z, precision=lax.Precision.HIGHEST)  166 us
    dot_general x128, matrix products, plane_potential(): jnp.dot(along_y * weight[None, :], along_z.T, precision=lax.Precision.HIG...  140 us
    mul x128, other arithmetic, plane_potential(): weight = gaussian(xcoord, plane_id.astype(jnp.float32)[None])[0] * charges  88.7 us
    dynamic_slice x128, local copies, waits for them, and re-layouts, on_device(): lax.map(lambda row_id: plane_potential(whole_plane(row_id), xcoord, along...  74.5 us
  transfers between devices with their start and end apart: 4, of which 3 were waited for; matrix products, arithmetic and copies ran while one was open for 0% of the time, Pallas kernels for 0%

commit v1 on v0

v1 whole, which is shorter than its diff:
```python
import functools
import math

import jax
import jax.numpy as jnp
from jax import lax
from jax.experimental import pallas as pl
from jax.experimental.pallas import tpu as pltpu
from jax.sharding import PartitionSpec as P

BS = 128
BAND = 7
SLOTS = 15
ROWS = 8
NBLOCKS = 1024
DEVICES = 128
GRID = 128
SPAN = ROWS * BS
GROUP = 32
RING = 4
ATOMS_DEV = 512
ATOMS_HERE = GROUP * ATOMS_DEV

COUPLE = 0.5
DENSITY_SCALE = 0.05
ROOT = math.sqrt(math.log2(math.e) / 8.0)

MESH = pl.DeviceIdType.MESH
F32 = jnp.float32
BF16 = jnp.bfloat16


def dot(a, b):
    return jnp.dot(a, b, preferred_element_type=F32)


def dot_nt(a, b):
    return lax.dot_general(a, b, (((1,), (1,)), ((), ())), preferred_element_type=F32)


def bell(points, centre):
    offset = points - centre
    return jnp.exp2(-(offset * offset))


def kernel(
    density, mask, slabs, cells, atoms_in, new_density, energies,
    dens, left, right, s_next, s_prev, pu_out, pd_out, pu_in, pd_in,
    atoms, tab_y, tab_z, lhs, pot_acc, pot_out, pot_in, rho, e_out, e_in,
    dens_sem, out_sem, gather_sem, own_sem, halo_send, halo_recv, part_send, part_recv,
    pot_send, pot_recv, rho_send, rho_recv, en_send, en_recv,
):
    g, r, c = lax.axis_index("grp"), lax.axis_index("row"), lax.axis_index("col")
    me = (g * 8 + r) * 4 + c
    mine = g * 8 + r

    def coords(index):
        return (index // 32, (index // 4) % 8, index % 4)

    after = coords((me + 1) % DEVICES)
    before = coords((me + DEVICES - 1) % DEVICES)

    def peer(k):
        slot = (mine + k) % GROUP
        return slot, (slot // 8, slot % 8, c)

    loads = [
        pltpu.make_async_copy(density.at[i], dens.at[i], dens_sem.at[i]) for i in range(ROWS)
    ]
    for load in loads:
        load.start()

    barrier = pltpu.get_barrier_semaphore()

    @pl.loop(1, GROUP)
    def _(k):
        pl.semaphore_signal(barrier, inc=1, device_id=peer(k)[1], device_id_type=MESH)

    for k in range(1, RING):
        pl.semaphore_signal(barrier, inc=1, device_id=(g, r, (c + k) % RING), device_id_type=MESH)
    pl.semaphore_signal(barrier, inc=1, device_id=after, device_id_type=MESH)
    pl.semaphore_signal(barrier, inc=1, device_id=before, device_id_type=MESH)
    pl.semaphore_wait(barrier, GROUP - 1 + RING - 1 + 2)

    own = pltpu.make_async_copy(atoms_in, atoms.at[mine], own_sem)
    own.start()

    @pl.loop(1, GROUP)
    def _(k):
        pltpu.make_async_remote_copy(
            atoms_in, atoms.at[mine], gather_sem.at[0], gather_sem.at[1],
            device_id=peer(k)[1], device_id_type=MESH,
        ).start()

    zero = jnp.zeros((BS, BS), BF16)
    for a in range(0, ROWS, 2):
        for i, j in ((a, a), (a, a + 1), (a + 1, a), (a + 1, a + 1)):
            if j >= i:
                left[i * BS:(i + 1) * BS, 2 * SPAN + j * BS:2 * SPAN + (j + 1) * BS] = zero
                right[i * BS:(i + 1) * BS, j * BS:(j + 1) * BS] = zero
            if j <= i:
                left[i * BS:(i + 1) * BS, j * BS:(j + 1) * BS] = zero
                right[2 * SPAN + i * BS:2 * SPAN + (i + 1) * BS, j * BS:(j + 1) * BS] = zero

    def valid(i, s):
        column = me * ROWS + (i + s - BAND)
        inside = jnp.logical_and(column >= 0, column < NBLOCKS)
        return (mask[i, s] * inside.astype(jnp.int32)).astype(F32)

    to_next, to_prev = [], []
    for i in range(ROWS):
        loads[i].wait()
        for s in range(SLOTS):
            k = i + s + 1
            block = (dens[i, s].astype(F32) * valid(i, s)).astype(BF16)
            left[i * BS:(i + 1) * BS, k * BS:(k + 1) * BS] = block
            if ROWS <= k < 2 * ROWS:
                right[SPAN + i * BS:SPAN + (i + 1) * BS, (k - ROWS) * BS:(k - ROWS + 1) * BS] = block
        here = pl.ds(i * BS, BS)
        if i > 0:
            copy = pltpu.make_async_remote_copy(
                left.at[here, pl.ds(2 * SPAN, i * BS)], right.at[here, pl.ds(0, i * BS)],
                halo_send.at[0, i], halo_recv.at[0, i], device_id=after, device_id_type=MESH,
            )
            copy.start()
            to_next.append(copy)
        if i < ROWS - 1:
            there = pl.ds((i + 1) * BS, (ROWS - 1 - i) * BS)
            copy = pltpu.make_async_remote_copy(
                left.at[here, there], right.at[pl.ds(2 * SPAN + i * BS, BS), there],
                halo_send.at[1, i], halo_recv.at[1, i], device_id=before, device_id_type=MESH,
            )
            copy.start()
            to_prev.append(copy)

    own.wait()
    others = atoms.at[pl.ds(0, GROUP - 1)]
    pltpu.make_async_copy(others, others, gather_sem.at[0]).wait()
    pltpu.make_async_copy(others, others, gather_sem.at[1]).wait()

    points = lax.broadcasted_iota(jnp.int32, (GRID, BS), 0).astype(F32) * ROOT
    planes = [slabs[(me - c) + p].astype(F32) * ROOT for p in range(RING)]
    pot_acc[...] = jnp.zeros_like(pot_acc)

    @pl.loop(0, GROUP)
    def _(slot):
        base = pl.multiple_of(slot * ATOMS_DEV, ATOMS_DEV)
        for j in range(4):
            at = pl.ds(base + j * BS, BS)
            centre = [atoms[slot, pl.ds(4 * d + j, 1), :] * (GRID * ROOT) for d in range(3)]
            charge = atoms[slot, pl.ds(12 + j, 1), :]
            along_y = bell(points, centre[1])
            high = along_y.astype(BF16)
            tab_y[0:GRID, at] = high
            tab_y[GRID:2 * GRID, at] = (along_y - high.astype(F32)).astype(BF16)
            along_z = bell(points, centre[2])
            tab_z[:, at] = along_z
            for p in range(RING):
                weight = bell(planes[p], centre[0]) * charge
                lhs[p * GRID:(p + 1) * GRID, j * BS:(j + 1) * BS] = (along_z * weight).astype(BF16)
        pot_acc[...] += dot_nt(lhs[...], tab_y[:, pl.ds(base, ATOMS_DEV)])

    for p in range(RING):
        part = pot_acc[p * GRID:(p + 1) * GRID, 0:GRID] + pot_acc[p * GRID:(p + 1) * GRID, GRID:2 * GRID]
        pot_out[p] = part
    pot_copies = []
    for k in range(1, RING):
        target = (c + k) % RING
        copy = pltpu.make_async_remote_copy(
            pot_out.at[target], pot_in.at[k], pot_send.at[k], pot_recv.at[k],
            device_id=(g, r, target), device_id_type=MESH,
        )
        copy.start()
        pot_copies.append(copy)
    potential = pot_out[c]
    for k, copy in zip(range(1, RING), pot_copies):
        copy.wait()
        potential = potential + pot_in[k]

    high = potential.astype(BF16)
    both = jnp.concatenate([high, (potential - high.astype(F32)).astype(BF16)], axis=1)
    cell_y = lax.shift_right_logical(cells[...], 7)
    cell_z = jnp.bitwise_and(cells[...], GRID - 1)
    height = lax.broadcasted_iota(jnp.int32, (GRID, BS), 0)
    eye = (height == lax.broadcasted_iota(jnp.int32, (GRID, BS), 1)).astype(F32)

    def hot(cell, i):
        return (height == cell[i:i + 1, :]).astype(F32)

    for i in range(ROWS):
        hot_y = hot(cell_y, i).astype(BF16)
        rows = dot(both, jnp.concatenate([hot_y, hot_y], axis=0))
        shift = COUPLE * jnp.sum(rows * hot(cell_z, i), axis=0, keepdims=True)
        block = ((dens[i, BAND].astype(F32) - shift * eye) * valid(i, BAND)).astype(BF16)
        left[i * BS:(i + 1) * BS, SPAN + i * BS:SPAN + (i + 1) * BS] = block
        right[SPAN + i * BS:SPAN + (i + 1) * BS, i * BS:(i + 1) * BS] = block

    for copy in to_next:
        copy.wait()
    for copy in to_prev:
        copy.wait()

    for a in range(0, ROWS, 2):
        rows = slice(a * BS, (a + 2) * BS)
        depth = (a + 2) * BS
        pu_out[rows, 0:depth] = dot(
            right[rows, 0:depth], right[SPAN:SPAN + depth, 0:depth]
        ).astype(BF16)
        pd_out[rows, a * BS:SPAN] = dot(
            right[2 * SPAN + a * BS:2 * SPAN + (a + 2) * BS, a * BS:SPAN],
            right[SPAN + a * BS:2 * SPAN, a * BS:SPAN],
        ).astype(BF16)
    parts = []
    for i in range(ROWS):
        here = pl.ds(i * BS, BS)
        if i > 0:
            there = pl.ds(0, i * BS)
            copy = pltpu.make_async_remote_copy(
                pu_out.at[here, there], pu_in.at[here, there],
                part_send.at[0, i], part_recv.at[0, i], device_id=before, device_id_type=MESH,
            )
            copy.start()
            parts.append(copy)
        if i < ROWS - 1:
            there = pl.ds((i + 1) * BS, (ROWS - 1 - i) * BS)
            copy = pltpu.make_async_remote_copy(
                pd_out.at[here, there], pd_in.at[here, there],
                part_send.at[1, i], part_recv.at[1, i], device_id=after, device_id_type=MESH,
            )
            copy.start()
            parts.append(copy)

    def middle(a, b):
        first, last = max(a, b) + 1, min(a, b) + 16
        window = slice(first * BS, (last + 1) * BS)
        total = dot(left[a * BS:(a + 2) * BS, window], right[window, b * BS:(b + 2) * BS])
        for i in (a, a + 1):
            for j in (b, b + 1):
                s = j - i + BAND
                held = left[i * BS:(i + 1) * BS, SPAN + j * BS:SPAN + (j + 1) * BS].astype(F32)
                square = total[(i - a) * BS:(i - a + 1) * BS, (j - b) * BS:(j - b + 1) * BS]
                dens[i, s] = ((2.0 * held - square) * valid(i, s)).astype(BF16)

    for a in range(0, ROWS, 2):
        middle(a, a)

    grid_here = jnp.zeros((GRID, GRID), F32)
    for i in range(ROWS):
        diagonal = jnp.sum(dens[i, BAND].astype(F32) * eye, axis=0, keepdims=True)
        spread = (hot(cell_z, i) * diagonal).astype(BF16)
        grid_here = grid_here + dot_nt(spread, hot(cell_y, i).astype(BF16))
    rho[0] = grid_here.astype(BF16)
    rho_copies = []
    for k in range(1, RING):
        copy = pltpu.make_async_remote_copy(
            rho.at[0], rho.at[k], rho_send.at[k], rho_recv.at[k],
            device_id=(g, r, (c + k) % RING), device_id_type=MESH,
        )
        copy.start()
        rho_copies.append(copy)

    for a in range(0, ROWS, 2):
        for b in range(0, ROWS, 2):
            if a != b:
                middle(a, b)
    for b in range(0, ROWS, 2):
        columns = slice(b * BS, (b + 2) * BS)
        rows = slice((b + 1) * BS, SPAN)
        s_next[rows, columns] = dot(
            left[rows, SPAN + b * BS:2 * SPAN],
            left[b * BS:SPAN, 2 * SPAN + b * BS:2 * SPAN + (b + 2) * BS],
        )
        rows = slice(0, (b + 1) * BS)
        s_prev[rows, columns] = dot(
            left[rows, SPAN:SPAN + (b + 2) * BS], left[0:(b + 2) * BS, b * BS:(b + 2) * BS]
        )

    for copy in rho_copies:
        copy.wait()

    order = [lax.rem(c - k + RING, RING) for k in range(RING)]
    mine_planes = [slabs[(me - c) + order[k]].astype(F32) * ROOT for k in range(RING)]
    weights = jnp.concatenate([rho[k] for k in range(RING)], axis=0)
    lhs[:, 0:GRID] = weights
    lhs[:, GRID:2 * GRID] = weights

    @pl.loop(0, GROUP)
    def _(k):
        slot = (mine + 1 + k) % GROUP
        base = pl.multiple_of(slot * ATOMS_DEV, ATOMS_DEV)
        inner = dot(lhs[:, 0:2 * GRID], tab_y[:, pl.ds(base, ATOMS_DEV)])
        for j in range(4):
            at = pl.ds(base + j * BS, BS)
            centre = atoms[slot, pl.ds(j, 1), :] * (GRID * ROOT)
            along_z = tab_z[:, at]
            total = jnp.zeros((1, BS), F32)
            for p in range(RING):
                piece = inner[p * GRID:(p + 1) * GRID, j * BS:(j + 1) * BS]
                total += bell(mine_planes[p], centre) * jnp.sum(piece * along_z, axis=0, keepdims=True)
            e_out[slot, pl.ds(j, 1), :] = total

        @pl.when(k < GROUP - 1)
        def _():
            pltpu.make_async_remote_copy(
                e_out.at[slot], e_in.at[mine], en_send, en_recv,
                device_id=(slot // 8, slot % 8, c), device_id_type=MESH,
            ).start()

    e_in[mine] = e_out[mine]

    for copy in parts:
        copy.wait()
    for i in range(ROWS):
        here = slice(i * BS, (i + 1) * BS)
        for j in range(ROWS):
            there = slice(j * BS, (j + 1) * BS)
            if j < i:
                s = j - i + SLOTS
                held = left[here, 2 * SPAN + j * BS:2 * SPAN + (j + 1) * BS].astype(F32)
                square = s_next[here, there] + pu_in[here, there].astype(F32)
                dens[i, s] = ((2.0 * held - square) * valid(i, s)).astype(BF16)
            if j > i:
                s = j - i - 1
                held = left[here, there].astype(F32)
                square = s_prev[here, there] + pd_in[here, there].astype(F32)
                dens[i, s] = ((2.0 * held - square) * valid(i, s)).astype(BF16)
        pltpu.make_async_copy(dens.at[i], new_density.at[i], out_sem.at[i]).start()

    others = e_out.at[pl.ds(0, GROUP - 1)]
    pltpu.make_async_copy(others, others, en_send).wait()
    pltpu.make_async_copy(others, others, en_recv).wait()
    energies[...] = jnp.sum(e_in[...], axis=0) * DENSITY_SCALE * atoms[mine, pl.ds(12, 4), :]
    for i in range(ROWS):
        pltpu.make_async_copy(dens.at[i], new_density.at[i], out_sem.at[i]).wait()


def on_device(density, block_mask, orbital_cell, slab_of_device, positions, charges):
    atoms = jnp.concatenate([positions.reshape(12, BS), charges.reshape(4, BS)], axis=0)
    dma = pltpu.SemaphoreType.DMA
    new_density, energies = pl.pallas_call(
        kernel,
        out_shape=(
            jax.ShapeDtypeStruct((ROWS, SLOTS, BS, BS), BF16),
            jax.ShapeDtypeStruct((4, BS), F32),
        ),
        in_specs=[
            pl.BlockSpec(memory_space=pl.ANY),
            pl.BlockSpec(memory_space=pltpu.SMEM),
            pl.BlockSpec(memory_space=pltpu.SMEM),
            pl.BlockSpec(memory_space=pltpu.VMEM),
            pl.BlockSpec(memory_space=pltpu.VMEM),
        ],
        out_specs=(pl.BlockSpec(memory_space=pl.ANY), pl.BlockSpec(memory_space=pltpu.VMEM)),
        scratch_shapes=[
            pltpu.VMEM((ROWS, SLOTS, BS, BS), BF16),
            pltpu.VMEM((SPAN, 3 * SPAN), BF16),
            pltpu.VMEM((3 * SPAN, SPAN), BF16),
            pltpu.VMEM((SPAN, SPAN), F32),
            pltpu.VMEM((SPAN, SPAN), F32),
            pltpu.VMEM((SPAN, SPAN), BF16),
            pltpu.VMEM((SPAN, SPAN), BF16),
            pltpu.VMEM((SPAN, SPAN), BF16),
            pltpu.VMEM((SPAN, SPAN), BF16),
            pltpu.VMEM((GROUP, 16, BS), F32),
            pltpu.VMEM((2 * GRID, ATOMS_HERE), BF16),
            pltpu.VMEM((GRID, ATOMS_HERE), F32),
            pltpu.VMEM((RING * GRID, ATOMS_DEV), BF16),
            pltpu.VMEM((RING * GRID, 2 * GRID), F32),
            pltpu.VMEM((RING, GRID, GRID), F32),
            pltpu.VMEM((RING, GRID, GRID), F32),
            pltpu.VMEM((RING, GRID, GRID), BF16),
            pltpu.VMEM((GROUP, 4, BS), F32),
            pltpu.VMEM((GROUP, 4, BS), F32),
            dma((ROWS,)),
            dma((ROWS,)),
            dma((2,)),
            dma,
            dma((2, ROWS)),
            dma((2, ROWS)),
            dma((2, ROWS)),
            dma((2, ROWS)),
            dma((RING,)),
            dma((RING,)),
            dma((RING,)),
            dma((RING,)),
            dma,
            dma,
        ],
        compiler_params=pltpu.CompilerParams(
            collective_id=0, has_side_effects=True, vmem_limit_bytes=60 * 1024 * 1024
        ),
        cost_estimate=pl.CostEstimate(flops=10**10, bytes_accessed=10**7, transcendentals=4 * 10**6),
        name="purify",
    )(density, block_mask, slab_of_device, orbital_cell.reshape(ROWS, BS), atoms)
    return new_density, energies.reshape(ATOMS_DEV)


def solution(mesh):
    in_specs = (
        P(("grp", "row", "col"), None, None, None),
        P(("grp", "row", "col"), None),
        P(("grp", "row", "col")),
        P(),
        P(None, ("grp", "row", "col")),
        P(("grp", "row", "col")),
    )
    out_specs = (P(("grp", "row", "col"), None, None, None), P(("grp", "row", "col")))
    return jax.shard_map(
        on_device, mesh=mesh, in_specs=in_specs, out_specs=out_specs, check_vma=False
    )
```

time: 2240 us -> 104 us (0.05)
  waiting for transfers between devices: 993 us -> 0 us
  loops' own time: 406 us -> 0 us
  matrix products: 326 us -> 0 us
  local copies, waits for them, and re-layouts: 328 us -> 5.87 us
  other arithmetic: 147 us -> 1.29 us
  Pallas kernels: 0 us -> 95.1 us
    reduce_scatter x1 -> x0, waiting for transfers between devices: 600 us -> none  [on_device(): lax.psum_scatter(lax.map(lambda row_id: plane_potential(whole_plane(row_i...]
    another operation x2 -> x0, loops' own time: 406 us -> none  [the longest x1 332 us: on_device(): lax.map(lambda row_id: plane_potential(whole_plane(row_id), xcoord, along...]
    dot_general x271 -> x0, matrix products: 326 us -> none  [the longest x128 166 us: plane_energy(): inner_sum = jnp.dot(rho_plane, along_z, precision=lax.Precision.HIGHEST)]
    all_gather x1 -> x0, waiting for transfers between devices: 320 us -> none  [on_device(): lax.all_gather(grid_density.astype(jnp.bfloat16), ('grp', 'row', 'col'),...]
    dynamic_slice x384 -> x0, local copies, waits for them, and re-layouts: 305 us -> none  [the longest x256 230 us: whole_plane(): slab_of_device[row_id // PLANES_DEV] * PLANES_DEV + row_id % PLANES_DEV]
    pallas_call x0 -> x1, Pallas kernels: none -> 95.1 us  [on_device(): pl.pallas_call(kernel, out_shape=(jax.ShapeDtypeStruct((ROWS, SLOTS, BS,...]
    mul x133 -> x0, other arithmetic: 94.5 us -> none  [the longest x128 88.7 us: plane_potential(): weight = gaussian(xcoord, plane_id.astype(jnp.float32)[None])[0] * charges]
    ppermute x2 -> x0, waiting for transfers between devices: 72.8 us -> none  [the longest x1 72.8 us: with_halo(): lax.ppermute(lax.slice_in_dim(block, block.shape[dim] - width, None, axis...]
  transfers between devices with their start and end apart: 4 -> 0, of which waited for: 3 -> 0; matrix products, arithmetic and copies ran while one was open for 0% -> 0% of each run, Pallas kernels for 0% -> 0%
where the time goes in v1:
time: 104 us; the launch traced here: 103 us
  Pallas kernels  95.1 us (91%)
  local copies, waits for them, and re-layouts  5.87 us (6%)
  other arithmetic  1.29 us (1%)
    pallas_call x1, Pallas kernels, on_device(): pl.pallas_call(kernel, out_shape=(jax.ShapeDtypeStruct((ROWS, SLOTS, BS,...  95.1 us
    unnamed x4, local copies, waits for them, and re-layouts  5.16 us

profile of v1, /device:TPU:1, one launch (start us, length us, event | category | flops | bytes accessed | tf_op | source)
XLA Modules:
  0.0 102.9 jit_solution(13531415661339224158)
XLA Ops:
  0.6 0.7 reshape.17
  1.3 1.3 %pad_maximum_fusion.atoms_in = f32[16,128]{1,0:T(8,128)} fusion(f32[4,128]{1,0:T(4,128)} %bitcast.3, f32[12,128]{1,0:T(8,128)S(1)} %reshape.17), kind=kLoop, calls=%fused_computation | loop fusion | flops 2048 | bytes 16384 | tf_op jit(solution)/shard_map/concatenate | solution.py:338
  2.6 95.1 %purify.1 = (bf16[8,15,128,128]{3,2,1,0:T(8,128)(2,1)}, f32[4,128]{1,0:T(4,128)}) custom-call(bf16[8,15,128,128]{3,2,1,0:T(8,128)(2,1)} %density.1, s32[8,15]{1,0:T(8,128)} %mask.1, s32[128]{0:T(128)} %slabs.1, s32[8,128]{1,0:T(8,128)} %bitcast.5, f32[16,128]{1,0:T(8,128)} %pad_maximum_fusion.atoms_in), custom_call_target="tpu_custom_call" | custom-call | flops 10000000000 | bytes 10000000 | tf_op jit(solution)/shard_map/purify/pallas_call | solution.py:340
  97.7 0.0 copy-start
  97.7 4.6 %copy.10 = bf16[8,15,128,128]{3,2,1,0:T(8,128)(2,1)} copy(bf16[8,15,128,128]{3,2,1,0:T(8,128)(2,1)} %get-tuple-element.8) | data formatting | bytes 7864320
  102.3 0.0 copy-done
  102.3 0.6 copy.11
Async XLA Ops:
  97.7 4.6 %copy-start = (f32[4,128]{1,0:T(4,128)S(1)}, f32[4,128]{1,0:T(4,128)}, u32[]{:S(2)}) copy-start(f32[4,128]{1,0:T(4,128)} %get-tuple-element.5) | copy-start | bytes 6148

commit v2 on v1

--- a/solution.py
+++ b/solution.py
@@ -44,15 +44,16 @@
 
 
 def kernel(
-    density, mask, slabs, cells, atoms_in, new_density, energies,
+    density, mask, slabs, cells, positions, charges, new_density, energies,
     dens, left, right, s_next, s_prev, pu_out, pd_out, pu_in, pd_in,
-    atoms, tab_y, tab_z, lhs, pot_acc, pot_out, pot_in, rho, e_out, e_in,
-    dens_sem, out_sem, gather_sem, own_sem, halo_send, halo_recv, part_send, part_recv,
+    atoms, diff, diff_in, tab_y, tab_z, lhs, pot_acc, pot_out, pot_in, rho, e_out, e_in,
+    dens_sem, out_sem, early_sem, diff_sem, gather_sem, halo_send, halo_recv, part_send, part_recv,
     pot_send, pot_recv, rho_send, rho_recv, en_send, en_recv,
 ):
     g, r, c = lax.axis_index("grp"), lax.axis_index("row"), lax.axis_index("col")
     me = (g * 8 + r) * 4 + c
-    mine = g * 8 + r
+    half, z = r // 4, r % 4
+    mine = (g * 2 + half) * 4 + c
 
     def coords(index):
         return (index // 32, (index // 4) % 8, index % 4)
@@ -60,15 +61,26 @@
     after = coords((me + 1) % DEVICES)
     before = coords((me + DEVICES - 1) % DEVICES)
 
+    def place(slot):
+        return (slot // 8, ((slot // 4) % 2) * 4 + z, slot % 4)
+
     def peer(k):
         slot = (mine + k) % GROUP
-        return slot, (slot // 8, slot % 8, c)
+        return slot, place(slot)
+
+    def ring(k):
+        return (g, half * 4 + (z + k) % RING, c)
 
     loads = [
         pltpu.make_async_copy(density.at[i], dens.at[i], dens_sem.at[i]) for i in range(ROWS)
     ]
-    for load in loads:
-        load.start()
+    outside_in = (7, 0, 6, 1, 5, 2, 4, 3)
+    for i in outside_in:
+        loads[i].start()
+    for j in range(4):
+        for d in range(3):
+            atoms[mine, pl.ds(4 * d + j, 1), :] = positions[d:d + 1, j * BS:(j + 1) * BS]
+        atoms[mine, pl.ds(12 + j, 1), :] = charges[j:j + 1, :]
 
     barrier = pltpu.get_barrier_semaphore()
 
@@ -77,18 +89,15 @@
         pl.semaphore_signal(barrier, inc=1, device_id=peer(k)[1], device_id_type=MESH)
 
     for k in range(1, RING):
-        pl.semaphore_signal(barrier, inc=1, device_id=(g, r, (c + k) % RING), device_id_type=MESH)
+        pl.semaphore_signal(barrier, inc=1, device_id=ring(k), device_id_type=MESH)
     pl.semaphore_signal(barrier, inc=1, device_id=after, device_id_type=MESH)
     pl.semaphore_signal(barrier, inc=1, device_id=before, device_id_type=MESH)
     pl.semaphore_wait(barrier, GROUP - 1 + RING - 1 + 2)
 
-    own = pltpu.make_async_copy(atoms_in, atoms.at[mine], own_sem)
-    own.start()
-
     @pl.loop(1, GROUP)
     def _(k):
         pltpu.make_async_remote_copy(
-            atoms_in, atoms.at[mine], gather_sem.at[0], gather_sem.at[1],
+            atoms.at[mine], atoms.at[mine], gather_sem.at[0], gather_sem.at[1],
             device_id=peer(k)[1], device_id_type=MESH,
         ).start()
 
@@ -107,8 +116,8 @@
         inside = jnp.logical_and(column >= 0, column < NBLOCKS)
         return (mask[i, s] * inside.astype(jnp.int32)).astype(F32)
 
-    to_next, to_prev = [], []
-    for i in range(ROWS):
+    to_next, to_prev = {}, {}
+    for i in outside_in:
         loads[i].wait()
         for s in range(SLOTS):
             k = i + s + 1
@@ -123,7 +132,7 @@
                 halo_send.at[0, i], halo_recv.at[0, i], device_id=after, device_id_type=MESH,
             )
             copy.start()
-            to_next.append(copy)
+            to_next[i] = copy
         if i < ROWS - 1:
             there = pl.ds((i + 1) * BS, (ROWS - 1 - i) * BS)
             copy = pltpu.make_async_remote_copy(
@@ -131,48 +140,91 @@
                 halo_send.at[1, i], halo_recv.at[1, i], device_id=before, device_id_type=MESH,
             )
             copy.start()
-            to_prev.append(copy)
-
-    own.wait()
+            to_prev[i] = copy
+
     others = atoms.at[pl.ds(0, GROUP - 1)]
     pltpu.make_async_copy(others, others, gather_sem.at[0]).wait()
     pltpu.make_async_copy(others, others, gather_sem.at[1]).wait()
 
     points = lax.broadcasted_iota(jnp.int32, (GRID, BS), 0).astype(F32) * ROOT
-    planes = [slabs[(me - c) + p].astype(F32) * ROOT for p in range(RING)]
+    first = me - 4 * z
+    planes = [slabs[first + 4 * p].astype(F32) * ROOT for p in range(RING)]
     pot_acc[...] = jnp.zeros_like(pot_acc)
 
-    @pl.loop(0, GROUP)
-    def _(slot):
-        base = pl.multiple_of(slot * ATOMS_DEV, ATOMS_DEV)
+    def tables(slot):
+        ys, ws = [], []
         for j in range(4):
-            at = pl.ds(base + j * BS, BS)
+            at = pl.ds(pl.multiple_of(slot * ATOMS_DEV + j * BS, BS), BS)
             centre = [atoms[slot, pl.ds(4 * d + j, 1), :] * (GRID * ROOT) for d in range(3)]
             charge = atoms[slot, pl.ds(12 + j, 1), :]
             along_y = bell(points, centre[1])
             high = along_y.astype(BF16)
+            low = (along_y - high.astype(F32)).astype(BF16)
             tab_y[0:GRID, at] = high
-            tab_y[GRID:2 * GRID, at] = (along_y - high.astype(F32)).astype(BF16)
+            tab_y[GRID:2 * GRID, at] = low
+            ys.append(jnp.concatenate([high, low], axis=0))
             along_z = bell(points, centre[2])
             tab_z[:, at] = along_z
-            for p in range(RING):
-                weight = bell(planes[p], centre[0]) * charge
-                lhs[p * GRID:(p + 1) * GRID, j * BS:(j + 1) * BS] = (along_z * weight).astype(BF16)
-        pot_acc[...] += dot_nt(lhs[...], tab_y[:, pl.ds(base, ATOMS_DEV)])
+            ws.append(jnp.concatenate([
+                (along_z * (bell(planes[p], centre[0]) * charge)).astype(BF16) for p in range(RING)
+            ], axis=0))
+        return jnp.concatenate(ws, axis=1), jnp.concatenate(ys, axis=1)
+
+    def partial_potential(start, stop):
+        @pl.loop(start, stop)
+        def _(t):
+            ones = tables(2 * t)
+            twos = tables(2 * t + 1)
+            pot_acc[...] += dot_nt(*ones) + dot_nt(*twos)
+
+    parts = []
+
+    def corners(rows_next, rows_prev):
+        for i in rows_next:
+            to_next[i].wait()
+            here, there = pl.ds(i * BS, BS), pl.ds(0, i * BS)
+            pu_out[here, there] = dot(
+                right[i * BS:(i + 1) * BS, 0:i * BS], right[SPAN:SPAN + i * BS, 0:i * BS]
+            ).astype(BF16)
+            copy = pltpu.make_async_remote_copy(
+                pu_out.at[here, there], pu_in.at[here, there],
+                part_send.at[0, i], part_recv.at[0, i], device_id=before, device_id_type=MESH,
+            )
+            copy.start()
+            parts.append(copy)
+        for i in rows_prev:
+            to_prev[i].wait()
+            start = (i + 1) * BS
+            here, there = pl.ds(i * BS, BS), pl.ds(start, SPAN - start)
+            pd_out[here, there] = dot(
+                right[2 * SPAN + i * BS:2 * SPAN + (i + 1) * BS, start:SPAN],
+                right[SPAN + start:2 * SPAN, start:SPAN],
+            ).astype(BF16)
+            copy = pltpu.make_async_remote_copy(
+                pd_out.at[here, there], pd_in.at[here, there],
+                part_send.at[1, i], part_recv.at[1, i], device_id=after, device_id_type=MESH,
+            )
+            copy.start()
+            parts.append(copy)
+
+    partial_potential(0, GROUP // 4)
+    corners((7, 6), (0, 1))
+    partial_potential(GROUP // 4, GROUP // 2)
 
     for p in range(RING):
         part = pot_acc[p * GRID:(p + 1) * GRID, 0:GRID] + pot_acc[p * GRID:(p + 1) * GRID, GRID:2 * GRID]
         pot_out[p] = part
     pot_copies = []
     for k in range(1, RING):
-        target = (c + k) % RING
+        target = (z + k) % RING
         copy = pltpu.make_async_remote_copy(
             pot_out.at[target], pot_in.at[k], pot_send.at[k], pot_recv.at[k],
-            device_id=(g, r, target), device_id_type=MESH,
+            device_id=ring(k), device_id_type=MESH,
         )
         copy.start()
         pot_copies.append(copy)
-    potential = pot_out[c]
+    corners((5, 4, 3, 2, 1), (2, 3, 4, 5, 6))
+    potential = pot_out[z]
     for k, copy in zip(range(1, RING), pot_copies):
         copy.wait()
         potential = potential + pot_in[k]
@@ -192,43 +244,18 @@
         rows = dot(both, jnp.concatenate([hot_y, hot_y], axis=0))
         shift = COUPLE * jnp.sum(rows * hot(cell_z, i), axis=0, keepdims=True)
         block = ((dens[i, BAND].astype(F32) - shift * eye) * valid(i, BAND)).astype(BF16)
+        plain = right[SPAN + i * BS:SPAN + (i + 1) * BS, i * BS:(i + 1) * BS].astype(F32)
+        diff[i:i + 1, :] = jnp.sum((block.astype(F32) - plain) * eye, axis=0, keepdims=True)
         left[i * BS:(i + 1) * BS, SPAN + i * BS:SPAN + (i + 1) * BS] = block
         right[SPAN + i * BS:SPAN + (i + 1) * BS, i * BS:(i + 1) * BS] = block
 
-    for copy in to_next:
-        copy.wait()
-    for copy in to_prev:
-        copy.wait()
-
-    for a in range(0, ROWS, 2):
-        rows = slice(a * BS, (a + 2) * BS)
-        depth = (a + 2) * BS
-        pu_out[rows, 0:depth] = dot(
-            right[rows, 0:depth], right[SPAN:SPAN + depth, 0:depth]
-        ).astype(BF16)
-        pd_out[rows, a * BS:SPAN] = dot(
-            right[2 * SPAN + a * BS:2 * SPAN + (a + 2) * BS, a * BS:SPAN],
-            right[SPAN + a * BS:2 * SPAN, a * BS:SPAN],
-        ).astype(BF16)
-    parts = []
-    for i in range(ROWS):
-        here = pl.ds(i * BS, BS)
-        if i > 0:
-            there = pl.ds(0, i * BS)
-            copy = pltpu.make_async_remote_copy(
-                pu_out.at[here, there], pu_in.at[here, there],
-                part_send.at[0, i], part_recv.at[0, i], device_id=before, device_id_type=MESH,
-            )
-            copy.start()
-            parts.append(copy)
-        if i < ROWS - 1:
-            there = pl.ds((i + 1) * BS, (ROWS - 1 - i) * BS)
-            copy = pltpu.make_async_remote_copy(
-                pd_out.at[here, there], pd_in.at[here, there],
-                part_send.at[1, i], part_recv.at[1, i], device_id=after, device_id_type=MESH,
-            )
-            copy.start()
-            parts.append(copy)
+    for k, target in ((0, after), (1, before)):
+        copy = pltpu.make_async_remote_copy(
+            diff, diff_in.at[k], diff_sem.at[0, k], diff_sem.at[1, k],
+            device_id=target, device_id_type=MESH,
+        )
+        copy.start()
+        parts.append(copy)
 
     def middle(a, b):
         first, last = max(a, b) + 1, min(a, b) + 16
@@ -254,7 +281,7 @@
     for k in range(1, RING):
         copy = pltpu.make_async_remote_copy(
             rho.at[0], rho.at[k], rho_send.at[k], rho_recv.at[k],
-            device_id=(g, r, (c + k) % RING), device_id_type=MESH,
+            device_id=ring(k), device_id_type=MESH,
         )
         copy.start()
         rho_copies.append(copy)
@@ -275,11 +302,19 @@
             left[rows, SPAN:SPAN + (b + 2) * BS], left[0:(b + 2) * BS, b * BS:(b + 2) * BS]
         )
 
+    early = [
+        pltpu.make_async_copy(
+            dens.at[i, pl.ds(BAND - i, ROWS)], new_density.at[i, pl.ds(BAND - i, ROWS)], early_sem.at[i]
+        )
+        for i in range(ROWS)
+    ]
+    for copy in early:
+        copy.start()
     for copy in rho_copies:
         copy.wait()
 
-    order = [lax.rem(c - k + RING, RING) for k in range(RING)]
-    mine_planes = [slabs[(me - c) + order[k]].astype(F32) * ROOT for k in range(RING)]
+    order = [(z - k + RING) % RING for k in range(RING)]
+    mine_planes = [slabs[first + 4 * order[k]].astype(F32) * ROOT for k in range(RING)]
     weights = jnp.concatenate([rho[k] for k in range(RING)], axis=0)
     lhs[:, 0:GRID] = weights
     lhs[:, GRID:2 * GRID] = weights
@@ -303,13 +338,14 @@
         def _():
             pltpu.make_async_remote_copy(
                 e_out.at[slot], e_in.at[mine], en_send, en_recv,
-                device_id=(slot // 8, slot % 8, c), device_id_type=MESH,
+                device_id=place(slot), device_id_type=MESH,
             ).start()
 
     e_in[mine] = e_out[mine]
 
     for copy in parts:
         copy.wait()
+    late = []
     for i in range(ROWS):
         here = slice(i * BS, (i + 1) * BS)
         for j in range(ROWS):
@@ -318,24 +354,29 @@
                 s = j - i + SLOTS
                 held = left[here, 2 * SPAN + j * BS:2 * SPAN + (j + 1) * BS].astype(F32)
                 square = s_next[here, there] + pu_in[here, there].astype(F32)
-                dens[i, s] = ((2.0 * held - square) * valid(i, s)).astype(BF16)
+                dens[i, s] = ((held * (2.0 - diff_in[1, j:j + 1, :]) - square) * valid(i, s)).astype(BF16)
             if j > i:
                 s = j - i - 1
                 held = left[here, there].astype(F32)
                 square = s_prev[here, there] + pd_in[here, there].astype(F32)
-                dens[i, s] = ((2.0 * held - square) * valid(i, s)).astype(BF16)
-        pltpu.make_async_copy(dens.at[i], new_density.at[i], out_sem.at[i]).start()
+                dens[i, s] = ((held * (2.0 - diff_in[0, j:j + 1, :]) - square) * valid(i, s)).astype(BF16)
+        for k, (start, size) in enumerate(((0, BAND - i), (SLOTS - i, i))):
+            if size:
+                copy = pltpu.make_async_copy(
+                    dens.at[i, pl.ds(start, size)], new_density.at[i, pl.ds(start, size)], out_sem.at[k, i]
+                )
+                copy.start()
+                late.append(copy)
 
     others = e_out.at[pl.ds(0, GROUP - 1)]
     pltpu.make_async_copy(others, others, en_send).wait()
     pltpu.make_async_copy(others, others, en_recv).wait()
     energies[...] = jnp.sum(e_in[...], axis=0) * DENSITY_SCALE * atoms[mine, pl.ds(12, 4), :]
-    for i in range(ROWS):
-        pltpu.make_async_copy(dens.at[i], new_density.at[i], out_sem.at[i]).wait()
+    for copy in early + late:
+        copy.wait()
 
 
 def on_device(density, block_mask, orbital_cell, slab_of_device, positions, charges):
-    atoms = jnp.concatenate([positions.reshape(12, BS), charges.reshape(4, BS)], axis=0)
     dma = pltpu.SemaphoreType.DMA
     new_density, energies = pl.pallas_call(
         kernel,
@@ -347,6 +388,7 @@
             pl.BlockSpec(memory_space=pl.ANY),
             pl.BlockSpec(memory_space=pltpu.SMEM),
             pl.BlockSpec(memory_space=pltpu.SMEM),
+            pl.BlockSpec(memory_space=pltpu.VMEM),
             pl.BlockSpec(memory_space=pltpu.VMEM),
             pl.BlockSpec(memory_space=pltpu.VMEM),
         ],
@@ -362,6 +404,8 @@
             pltpu.VMEM((SPAN, SPAN), BF16),
             pltpu.VMEM((SPAN, SPAN), BF16),
             pltpu.VMEM((GROUP, 16, BS), F32),
+            pltpu.VMEM((ROWS, BS), F32),
+            pltpu.VMEM((2, ROWS, BS), F32),
             pltpu.VMEM((2 * GRID, ATOMS_HERE), BF16),
             pltpu.VMEM((GRID, ATOMS_HERE), F32),
             pltpu.VMEM((RING * GRID, ATOMS_DEV), BF16),
@@ -372,9 +416,10 @@
             pltpu.VMEM((GROUP, 4, BS), F32),
             pltpu.VMEM((GROUP, 4, BS), F32),
             dma((ROWS,)),
+            dma((2, ROWS)),
             dma((ROWS,)),
+            dma((2, 2)),
             dma((2,)),
-            dma,
             dma((2, ROWS)),
             dma((2, ROWS)),
             dma((2, ROWS)),
@@ -391,7 +436,7 @@
         ),
         cost_estimate=pl.CostEstimate(flops=10**10, bytes_accessed=10**7, transcendentals=4 * 10**6),
         name="purify",
-    )(density, block_mask, slab_of_device, orbital_cell.reshape(ROWS, BS), atoms)
+    )(density, block_mask, slab_of_device, orbital_cell.reshape(ROWS, BS), positions, charges.reshape(4, BS))
     return new_density, energies.reshape(ATOMS_DEV)
 
 

time: 104 us -> 85.6 us (0.82)
  Pallas kernels: 95.1 us -> 79.6 us
  other arithmetic: 1.29 us -> 0 us
    pallas_call x1, Pallas kernels: 95.1 us -> 79.6 us  [on_device(): pl.pallas_call(kernel, out_shape=(jax.ShapeDtypeStruct((ROWS, SLOTS, BS,...]
    concatenate x1 -> x0, other arithmetic: 1.29 us -> none  [on_device(): jnp.concatenate([positions.reshape(12, BS), charges.reshape(4, BS)], axis=0)]
where the time goes in v2:
time: 85.6 us; the launch traced here: 85.4 us
  Pallas kernels  79.6 us (93%)
  local copies, waits for them, and re-layouts  5.16 us (6%)
    pallas_call x1, Pallas kernels, on_device(): pl.pallas_call(kernel, out_shape=(jax.ShapeDtypeStruct((ROWS, SLOTS, BS,...  79.6 us
    unnamed x4, local copies, waits for them, and re-layouts  5.16 us

profile of v2, /device:TPU:1, one launch (start us, length us, event | category | flops | bytes accessed | tf_op | source)
XLA Modules:
  0.0 85.4 jit_solution(9021826026634107571)
XLA Ops:
  0.6 79.6 %purify.1 = (bf16[8,15,128,128]{3,2,1,0:T(8,128)(2,1)}, f32[4,128]{1,0:T(4,128)}) custom-call(bf16[8,15,128,128]{3,2,1,0:T(8,128)(2,1)} %density.1, s32[8,15]{1,0:T(8,128)} %mask.1, s32[128]{0:T(128)} %slabs.1, s32[8,128]{1,0:T(8,128)} %bitcast.4, f32[3,512]{1,0:T(4,128)} %positions.1, f32[4,128]{1,0:T(4,128)} %bitcast.5), custom_call_target="tpu_custom_call" | custom-call | flops 10000000000 | bytes 10000000 | tf_op jit(solution)/shard_map/purify/pallas_call | solution.py:381
  80.3 0.0 copy-start
  80.3 4.6 %copy.10 = bf16[8,15,128,128]{3,2,1,0:T(8,128)(2,1)} copy(bf16[8,15,128,128]{3,2,1,0:T(8,128)(2,1)} %get-tuple-element.8) | data formatting | bytes 7864320
  84.8 0.0 copy-done
  84.9 0.6 copy.11
Async XLA Ops:
  80.3 4.6 %copy-start = (f32[4,128]{1,0:T(4,128)S(1)}, f32[4,128]{1,0:T(4,128)}, u32[]{:S(2)}) copy-start(f32[4,128]{1,0:T(4,128)} %get-tuple-element.5) | copy-start | bytes 6148

commit v3 on v2

--- a/solution.py
+++ b/solution.py
@@ -44,10 +44,10 @@
 
 
 def kernel(
-    density, mask, slabs, cells, positions, charges, new_density, energies,
-    dens, left, right, s_next, s_prev, pu_out, pd_out, pu_in, pd_in,
+    density, mask, slabs, cells, positions, charges, dens, energies,
+    left, right, outer, pu_out, pd_out, pu_in, pd_in,
     atoms, diff, diff_in, tab_y, tab_z, lhs, pot_acc, pot_out, pot_in, rho, e_out, e_in,
-    dens_sem, out_sem, early_sem, diff_sem, gather_sem, halo_send, halo_recv, part_send, part_recv,
+    dens_sem, diff_sem, gather_sem, halo_send, halo_recv, part_send, part_recv,
     pot_send, pot_recv, rho_send, rho_recv, en_send, en_recv,
 ):
     g, r, c = lax.axis_index("grp"), lax.axis_index("row"), lax.axis_index("col")
@@ -177,39 +177,41 @@
             twos = tables(2 * t + 1)
             pot_acc[...] += dot_nt(*ones) + dot_nt(*twos)
 
-    parts = []
-
-    def corners(rows_next, rows_prev):
-        for i in rows_next:
-            to_next[i].wait()
-            here, there = pl.ds(i * BS, BS), pl.ds(0, i * BS)
-            pu_out[here, there] = dot(
-                right[i * BS:(i + 1) * BS, 0:i * BS], right[SPAN:SPAN + i * BS, 0:i * BS]
-            ).astype(BF16)
-            copy = pltpu.make_async_remote_copy(
-                pu_out.at[here, there], pu_in.at[here, there],
-                part_send.at[0, i], part_recv.at[0, i], device_id=before, device_id_type=MESH,
-            )
+    pairs = []
+
+    def corners(n):
+        i = BAND - n
+        to_next[i].wait()
+        here, there = pl.ds(i * BS, BS), pl.ds(0, i * BS)
+        pu_out[here, there] = dot(
+            right[i * BS:(i + 1) * BS, 0:i * BS], right[SPAN:SPAN + i * BS, 0:i * BS]
+        ).astype(BF16)
+        up = pltpu.make_async_remote_copy(
+            pu_out.at[here, there], pu_in.at[here, there],
+            part_send.at[0, i], part_recv.at[0, i], device_id=before, device_id_type=MESH,
+        )
+        to_prev[n].wait()
+        start = (n + 1) * BS
+        here, there = pl.ds(n * BS, BS), pl.ds(start, SPAN - start)
+        pd_out[here, there] = dot(
+            right[2 * SPAN + n * BS:2 * SPAN + (n + 1) * BS, start:SPAN],
+            right[SPAN + start:2 * SPAN, start:SPAN],
+        ).astype(BF16)
+        down = pltpu.make_async_remote_copy(
+            pd_out.at[here, there], pd_in.at[here, there],
+            part_send.at[1, n], part_recv.at[1, n], device_id=after, device_id_type=MESH,
+        )
+        pairs.append((up, down))
+
+    def start_pair(n):
+        for copy in pairs[n]:
             copy.start()
-            parts.append(copy)
-        for i in rows_prev:
-            to_prev[i].wait()
-            start = (i + 1) * BS
-            here, there = pl.ds(i * BS, BS), pl.ds(start, SPAN - start)
-            pd_out[here, there] = dot(
-                right[2 * SPAN + i * BS:2 * SPAN + (i + 1) * BS, start:SPAN],
-                right[SPAN + start:2 * SPAN, start:SPAN],
-            ).astype(BF16)
-            copy = pltpu.make_async_remote_copy(
-                pd_out.at[here, there], pd_in.at[here, there],
-                part_send.at[1, i], part_recv.at[1, i], device_id=after, device_id_type=MESH,
-            )
-            copy.start()
-            parts.append(copy)
-
-    partial_potential(0, GROUP // 4)
-    corners((7, 6), (0, 1))
-    partial_potential(GROUP // 4, GROUP // 2)
+
+    def sent_pair(n):
+        for copy in pairs[n]:
+            copy.wait_send()
+
+    partial_potential(0, GROUP // 2)
 
     for p in range(RING):
         part = pot_acc[p * GRID:(p + 1) * GRID, 0:GRID] + pot_acc[p * GRID:(p + 1) * GRID, GRID:2 * GRID]
@@ -223,7 +225,10 @@
         )
         copy.start()
         pot_copies.append(copy)
-    corners((5, 4, 3, 2, 1), (2, 3, 4, 5, 6))
+    corners(0)
+    start_pair(0)
+    for n in range(1, BAND):
+        corners(n)
     potential = pot_out[z]
     for k, copy in zip(range(1, RING), pot_copies):
         copy.wait()
@@ -249,13 +254,14 @@
         left[i * BS:(i + 1) * BS, SPAN + i * BS:SPAN + (i + 1) * BS] = block
         right[SPAN + i * BS:SPAN + (i + 1) * BS, i * BS:(i + 1) * BS] = block
 
+    diff_copies = []
     for k, target in ((0, after), (1, before)):
         copy = pltpu.make_async_remote_copy(
             diff, diff_in.at[k], diff_sem.at[0, k], diff_sem.at[1, k],
             device_id=target, device_id_type=MESH,
         )
         copy.start()
-        parts.append(copy)
+        diff_copies.append(copy)
 
     def middle(a, b):
         first, last = max(a, b) + 1, min(a, b) + 16
@@ -285,6 +291,8 @@
         )
         copy.start()
         rho_copies.append(copy)
+    start_pair(1)
+    start_pair(2)
 
     for a in range(0, ROWS, 2):
         for b in range(0, ROWS, 2):
@@ -293,23 +301,15 @@
     for b in range(0, ROWS, 2):
         columns = slice(b * BS, (b + 2) * BS)
         rows = slice((b + 1) * BS, SPAN)
-        s_next[rows, columns] = dot(
+        outer[rows, columns] = dot(
             left[rows, SPAN + b * BS:2 * SPAN],
             left[b * BS:SPAN, 2 * SPAN + b * BS:2 * SPAN + (b + 2) * BS],
         )
         rows = slice(0, (b + 1) * BS)
-        s_prev[rows, columns] = dot(
+        outer[rows, columns] = dot(
             left[rows, SPAN:SPAN + (b + 2) * BS], left[0:(b + 2) * BS, b * BS:(b + 2) * BS]
         )
 
-    early = [
-        pltpu.make_async_copy(
-            dens.at[i, pl.ds(BAND - i, ROWS)], new_density.at[i, pl.ds(BAND - i, ROWS)], early_sem.at[i]
-        )
-        for i in range(ROWS)
-    ]
-    for copy in early:
-        copy.start()
     for copy in rho_copies:
         copy.wait()
 
@@ -334,6 +334,12 @@
                 total += bell(mine_planes[p], centre) * jnp.sum(piece * along_z, axis=0, keepdims=True)
             e_out[slot, pl.ds(j, 1), :] = total
 
+        for when, n in ((4, 3), (12, 4), (20, 5), (26, 6)):
+            @pl.when(k == when)
+            def _(n=n):
+                sent_pair(n - 2)
+                start_pair(n)
+
         @pl.when(k < GROUP - 1)
         def _():
             pltpu.make_async_remote_copy(
@@ -343,37 +349,35 @@
 
     e_in[mine] = e_out[mine]
 
-    for copy in parts:
+    for copy in diff_copies:
         copy.wait()
-    late = []
-    for i in range(ROWS):
+    for n in range(BAND):
+        up, down = pairs[n]
+        if n == 0 or n > 4:
+            up.wait_send()
+            down.wait_send()
+        up.wait_recv()
+        i = BAND - n
         here = slice(i * BS, (i + 1) * BS)
-        for j in range(ROWS):
+        for j in range(i):
             there = slice(j * BS, (j + 1) * BS)
-            if j < i:
-                s = j - i + SLOTS
-                held = left[here, 2 * SPAN + j * BS:2 * SPAN + (j + 1) * BS].astype(F32)
-                square = s_next[here, there] + pu_in[here, there].astype(F32)
-                dens[i, s] = ((held * (2.0 - diff_in[1, j:j + 1, :]) - square) * valid(i, s)).astype(BF16)
-            if j > i:
-                s = j - i - 1
-                held = left[here, there].astype(F32)
-                square = s_prev[here, there] + pd_in[here, there].astype(F32)
-                dens[i, s] = ((held * (2.0 - diff_in[0, j:j + 1, :]) - square) * valid(i, s)).astype(BF16)
-        for k, (start, size) in enumerate(((0, BAND - i), (SLOTS - i, i))):
-            if size:
-                copy = pltpu.make_async_copy(
-                    dens.at[i, pl.ds(start, size)], new_density.at[i, pl.ds(start, size)], out_sem.at[k, i]
-                )
-                copy.start()
-                late.append(copy)
+            s = j - i + SLOTS
+            held = left[here, 2 * SPAN + j * BS:2 * SPAN + (j + 1) * BS].astype(F32)
+            square = outer[here, there] + pu_in[here, there].astype(F32)
+            dens[i, s] = ((held * (2.0 - diff_in[1, j:j + 1, :]) - square) * valid(i, s)).astype(BF16)
+        down.wait_recv()
+        here = slice(n * BS, (n + 1) * BS)
+        for j in range(n + 1, ROWS):
+            there = slice(j * BS, (j + 1) * BS)
+            s = j - n - 1
+            held = left[here, there].astype(F32)
+            square = outer[here, there] + pd_in[here, there].astype(F32)
+            dens[n, s] = ((held * (2.0 - diff_in[0, j:j + 1, :]) - square) * valid(n, s)).astype(BF16)
 
     others = e_out.at[pl.ds(0, GROUP - 1)]
     pltpu.make_async_copy(others, others, en_send).wait()
     pltpu.make_async_copy(others, others, en_recv).wait()
     energies[...] = jnp.sum(e_in[...], axis=0) * DENSITY_SCALE * atoms[mine, pl.ds(12, 4), :]
-    for copy in early + late:
-        copy.wait()
 
 
 def on_device(density, block_mask, orbital_cell, slab_of_device, positions, charges):
@@ -381,8 +385,8 @@
     new_density, energies = pl.pallas_call(
         kernel,
         out_shape=(
-            jax.ShapeDtypeStruct((ROWS, SLOTS, BS, BS), BF16),
-            jax.ShapeDtypeStruct((4, BS), F32),
+            pltpu.VMEM((ROWS, SLOTS, BS, BS), BF16),
+            pltpu.VMEM((4, BS), F32),
         ),
         in_specs=[
             pl.BlockSpec(memory_space=pl.ANY),
@@ -392,12 +396,10 @@
             pl.BlockSpec(memory_space=pltpu.VMEM),
             pl.BlockSpec(memory_space=pltpu.VMEM),
         ],
-        out_specs=(pl.BlockSpec(memory_space=pl.ANY), pl.BlockSpec(memory_space=pltpu.VMEM)),
+        out_specs=(pl.BlockSpec(memory_space=pltpu.VMEM), pl.BlockSpec(memory_space=pltpu.VMEM)),
         scratch_shapes=[
-            pltpu.VMEM((ROWS, SLOTS, BS, BS), BF16),
             pltpu.VMEM((SPAN, 3 * SPAN), BF16),
             pltpu.VMEM((3 * SPAN, SPAN), BF16),
-            pltpu.VMEM((SPAN, SPAN), F32),
             pltpu.VMEM((SPAN, SPAN), F32),
             pltpu.VMEM((SPAN, SPAN), BF16),
             pltpu.VMEM((SPAN, SPAN), BF16),
@@ -416,8 +418,6 @@
             pltpu.VMEM((GROUP, 4, BS), F32),
             pltpu.VMEM((GROUP, 4, BS), F32),
             dma((ROWS,)),
-            dma((2, ROWS)),
-            dma((ROWS,)),
             dma((2, 2)),
             dma((2,)),
             dma((2, ROWS)),
@@ -432,7 +432,7 @@
             dma,
         ],
         compiler_params=pltpu.CompilerParams(
-            collective_id=0, has_side_effects=True, vmem_limit_bytes=60 * 1024 * 1024
+            collective_id=0, has_side_effects=True, vmem_limit_bytes=52 * 1024 * 1024
         ),
         cost_estimate=pl.CostEstimate(flops=10**10, bytes_accessed=10**7, transcendentals=4 * 10**6),
         name="purify",

time: 85.6 us -> 78.4 us (0.916)
  Pallas kernels: 79.6 us -> 75 us
  local copies, waits for them, and re-layouts: 5.16 us -> 2.5 us
    pallas_call x1, Pallas kernels: 79.6 us -> 75 us  [on_device(): pl.pallas_call(kernel, out_shape=(pltpu.VMEM((ROWS, SLOTS, BS, BS), BF16)...]
    unnamed x4 -> x2, local copies, waits for them, and re-layouts: 5.16 us -> 2.5 us
where the time goes in v3:
time: 78.4 us; the launch traced here: 78.1 us
  Pallas kernels  75 us (96%)
  local copies, waits for them, and re-layouts  2.5 us (3%)
    pallas_call x1, Pallas kernels, on_device(): pl.pallas_call(kernel, out_shape=(pltpu.VMEM((ROWS, SLOTS, BS, BS), BF16)...  75 us
    unnamed x2, local copies, waits for them, and re-layouts  2.5 us

profile of v3, /device:TPU:1, one launch (start us, length us, event | category | flops | bytes accessed | tf_op | source)
XLA Modules:
  0.0 78.1 jit_solution(9730228476955470607)
XLA Ops:
  0.6 75.0 %purify.1 = (bf16[8,15,128,128]{3,2,1,0:T(8,128)(2,1)S(1)}, f32[4,128]{1,0:T(4,128)S(1)}) custom-call(bf16[8,15,128,128]{3,2,1,0:T(8,128)(2,1)} %density.1, s32[8,15]{1,0:T(8,128)} %mask.1, s32[128]{0:T(128)} %slabs.1, s32[8,128]{1,0:T(8,128)} %bitcast.4, f32[3,512]{1,0:T(4,128)} %positions.1, f32[4,128]{1,0:T(4,128)} %bitcast.5), custom_call_target="tpu_custom_call" | custom-call | flops 10000000000 | bytes 10000000 | tf_op jit(solution)/shard_map/purify/pallas_call | solution.py:385
  75.6 1.9 %copy.10 = bf16[8,15,128,128]{3,2,1,0:T(8,128)(2,1)} copy(bf16[8,15,128,128]{3,2,1,0:T(8,128)(2,1)S(1)} %get-tuple-element.6) | data formatting | bytes 7864320
  77.6 0.6 copy.11

commit v4 on v3

--- a/solution.py
+++ b/solution.py
@@ -46,8 +46,8 @@
 def kernel(
     density, mask, slabs, cells, positions, charges, dens, energies,
     left, right, outer, pu_out, pd_out, pu_in, pd_in,
-    atoms, diff, diff_in, tab_y, tab_z, lhs, pot_acc, pot_out, pot_in, rho, e_out, e_in,
-    dens_sem, diff_sem, gather_sem, halo_send, halo_recv, part_send, part_recv,
+    atoms, tab_y, tab_z, lhs, pot_acc, pot_out, pot_in, rho, e_out, e_in,
+    dens_sem, gather_sem, halo_send, halo_recv, part_send, part_recv,
     pot_send, pot_recv, rho_send, rho_recv, en_send, en_recv,
 ):
     g, r, c = lax.axis_index("grp"), lax.axis_index("row"), lax.axis_index("col")
@@ -181,7 +181,6 @@
 
     def corners(n):
         i = BAND - n
-        to_next[i].wait()
         here, there = pl.ds(i * BS, BS), pl.ds(0, i * BS)
         pu_out[here, there] = dot(
             right[i * BS:(i + 1) * BS, 0:i * BS], right[SPAN:SPAN + i * BS, 0:i * BS]
@@ -190,7 +189,6 @@
             pu_out.at[here, there], pu_in.at[here, there],
             part_send.at[0, i], part_recv.at[0, i], device_id=before, device_id_type=MESH,
         )
-        to_prev[n].wait()
         start = (n + 1) * BS
         here, there = pl.ds(n * BS, BS), pl.ds(start, SPAN - start)
         pd_out[here, there] = dot(
@@ -207,9 +205,9 @@
         for copy in pairs[n]:
             copy.start()
 
-    def sent_pair(n):
-        for copy in pairs[n]:
-            copy.wait_send()
+    def halo_pair(n):
+        to_next[BAND - n].wait()
+        to_prev[n].wait()
 
     partial_potential(0, GROUP // 2)
 
@@ -225,10 +223,6 @@
         )
         copy.start()
         pot_copies.append(copy)
-    corners(0)
-    start_pair(0)
-    for n in range(1, BAND):
-        corners(n)
     potential = pot_out[z]
     for k, copy in zip(range(1, RING), pot_copies):
         copy.wait()
@@ -249,19 +243,14 @@
         rows = dot(both, jnp.concatenate([hot_y, hot_y], axis=0))
         shift = COUPLE * jnp.sum(rows * hot(cell_z, i), axis=0, keepdims=True)
         block = ((dens[i, BAND].astype(F32) - shift * eye) * valid(i, BAND)).astype(BF16)
-        plain = right[SPAN + i * BS:SPAN + (i + 1) * BS, i * BS:(i + 1) * BS].astype(F32)
-        diff[i:i + 1, :] = jnp.sum((block.astype(F32) - plain) * eye, axis=0, keepdims=True)
         left[i * BS:(i + 1) * BS, SPAN + i * BS:SPAN + (i + 1) * BS] = block
         right[SPAN + i * BS:SPAN + (i + 1) * BS, i * BS:(i + 1) * BS] = block
 
-    diff_copies = []
-    for k, target in ((0, after), (1, before)):
-        copy = pltpu.make_async_remote_copy(
-            diff, diff_in.at[k], diff_sem.at[0, k], diff_sem.at[1, k],
-            device_id=target, device_id_type=MESH,
-        )
-        copy.start()
-        diff_copies.append(copy)
+    halo_pair(0)
+    corners(0)
+    for n in range(1, BAND):
+        halo_pair(n)
+    start_pair(0)
 
     def middle(a, b):
         first, last = max(a, b) + 1, min(a, b) + 16
@@ -291,8 +280,10 @@
         )
         copy.start()
         rho_copies.append(copy)
-    start_pair(1)
-    start_pair(2)
+    for n in range(1, BAND):
+        corners(n)
+        if n < 3:
+            start_pair(n)
 
     for a in range(0, ROWS, 2):
         for b in range(0, ROWS, 2):
@@ -312,6 +303,9 @@
 
     for copy in rho_copies:
         copy.wait()
+
+    for n in range(3, BAND):
+        start_pair(n)
 
     order = [(z - k + RING) % RING for k in range(RING)]
     mine_planes = [slabs[first + 4 * order[k]].astype(F32) * ROOT for k in range(RING)]
@@ -334,12 +328,6 @@
                 total += bell(mine_planes[p], centre) * jnp.sum(piece * along_z, axis=0, keepdims=True)
             e_out[slot, pl.ds(j, 1), :] = total
 
-        for when, n in ((4, 3), (12, 4), (20, 5), (26, 6)):
-            @pl.when(k == when)
-            def _(n=n):
-                sent_pair(n - 2)
-                start_pair(n)
-
         @pl.when(k < GROUP - 1)
         def _():
             pltpu.make_async_remote_copy(
@@ -349,14 +337,9 @@
 
     e_in[mine] = e_out[mine]
 
-    for copy in diff_copies:
-        copy.wait()
     for n in range(BAND):
         up, down = pairs[n]
-        if n == 0 or n > 4:
-            up.wait_send()
-            down.wait_send()
-        up.wait_recv()
+        up.wait()
         i = BAND - n
         here = slice(i * BS, (i + 1) * BS)
         for j in range(i):
@@ -364,15 +347,15 @@
             s = j - i + SLOTS
             held = left[here, 2 * SPAN + j * BS:2 * SPAN + (j + 1) * BS].astype(F32)
             square = outer[here, there] + pu_in[here, there].astype(F32)
-            dens[i, s] = ((held * (2.0 - diff_in[1, j:j + 1, :]) - square) * valid(i, s)).astype(BF16)
-        down.wait_recv()
+            dens[i, s] = ((2.0 * held - square) * valid(i, s)).astype(BF16)
+        down.wait()
         here = slice(n * BS, (n + 1) * BS)
         for j in range(n + 1, ROWS):
             there = slice(j * BS, (j + 1) * BS)
             s = j - n - 1
             held = left[here, there].astype(F32)
             square = outer[here, there] + pd_in[here, there].astype(F32)
-            dens[n, s] = ((held * (2.0 - diff_in[0, j:j + 1, :]) - square) * valid(n, s)).astype(BF16)
+            dens[n, s] = ((2.0 * held - square) * valid(n, s)).astype(BF16)
 
     others = e_out.at[pl.ds(0, GROUP - 1)]
     pltpu.make_async_copy(others, others, en_send).wait()
@@ -406,8 +389,6 @@
             pltpu.VMEM((SPAN, SPAN), BF16),
             pltpu.VMEM((SPAN, SPAN), BF16),
             pltpu.VMEM((GROUP, 16, BS), F32),
-            pltpu.VMEM((ROWS, BS), F32),
-            pltpu.VMEM((2, ROWS, BS), F32),
             pltpu.VMEM((2 * GRID, ATOMS_HERE), BF16),
             pltpu.VMEM((GRID, ATOMS_HERE), F32),
             pltpu.VMEM((RING * GRID, ATOMS_DEV), BF16),
@@ -418,7 +399,6 @@
             pltpu.VMEM((GROUP, 4, BS), F32),
             pltpu.VMEM((GROUP, 4, BS), F32),
             dma((ROWS,)),
-            dma((2, 2)),
             dma((2,)),
             dma((2, ROWS)),
             dma((2, ROWS)),

time: 78.4 us -> 77.5 us (0.989); the launches traced: 78.1 us -> 76.3 us
  Pallas kernels: 75 us -> 73.1 us
    pallas_call x1, Pallas kernels: 75 us -> 73.1 us  [on_device(): pl.pallas_call(kernel, out_shape=(pltpu.VMEM((ROWS, SLOTS, BS, BS), BF16)...]
where the time goes in v4:
time: 77.5 us; the launch traced here: 76.3 us
  Pallas kernels  73.1 us (94%)
  local copies, waits for them, and re-layouts  2.5 us (3%)
    pallas_call x1, Pallas kernels, on_device(): pl.pallas_call(kernel, out_shape=(pltpu.VMEM((ROWS, SLOTS, BS, BS), BF16)...  73.1 us
    unnamed x2, local copies, waits for them, and re-layouts  2.5 us

profile of v4, /device:TPU:1, one launch (start us, length us, event | category | flops | bytes accessed | tf_op | source)
XLA Modules:
  0.0 76.3 jit_solution(18262107329727720601)
XLA Ops:
  0.6 73.1 %purify.1 = (bf16[8,15,128,128]{3,2,1,0:T(8,128)(2,1)S(1)}, f32[4,128]{1,0:T(4,128)S(1)}) custom-call(bf16[8,15,128,128]{3,2,1,0:T(8,128)(2,1)} %density.1, s32[8,15]{1,0:T(8,128)} %mask.1, s32[128]{0:T(128)} %slabs.1, s32[8,128]{1,0:T(8,128)} %bitcast.4, f32[3,512]{1,0:T(4,128)} %positions.1, f32[4,128]{1,0:T(4,128)} %bitcast.5), custom_call_target="tpu_custom_call" | custom-call | flops 10000000000 | bytes 10000000 | tf_op jit(solution)/shard_map/purify/pallas_call | solution.py:368
  73.8 1.9 %copy.10 = bf16[8,15,128,128]{3,2,1,0:T(8,128)(2,1)} copy(bf16[8,15,128,128]{3,2,1,0:T(8,128)(2,1)S(1)} %get-tuple-element.6) | data formatting | bytes 7864320
  75.7 0.6 copy.11

commit v5 on v4

--- a/solution.py
+++ b/solution.py
@@ -282,8 +282,10 @@
         rho_copies.append(copy)
     for n in range(1, BAND):
         corners(n)
-        if n < 3:
-            start_pair(n)
+    for copy in rho_copies:
+        copy.wait()
+    for n in range(1, BAND):
+        start_pair(n)
 
     for a in range(0, ROWS, 2):
         for b in range(0, ROWS, 2):
@@ -301,11 +303,6 @@
             left[rows, SPAN:SPAN + (b + 2) * BS], left[0:(b + 2) * BS, b * BS:(b + 2) * BS]
         )
 
-    for copy in rho_copies:
-        copy.wait()
-
-    for n in range(3, BAND):
-        start_pair(n)
 
     order = [(z - k + RING) % RING for k in range(RING)]
     mine_planes = [slabs[first + 4 * order[k]].astype(F32) * ROOT for k in range(RING)]

time: 77.5 us -> 71.3 us (0.920)
  Pallas kernels: 73.1 us -> 67.1 us
    pallas_call x1, Pallas kernels: 73.1 us -> 67.1 us  [on_device(): pl.pallas_call(kernel, out_shape=(pltpu.VMEM((ROWS, SLOTS, BS, BS), BF16)...]
where the time goes in v5:
time: 71.3 us; the launch traced here: 70.2 us
  Pallas kernels  67.1 us (94%)
  local copies, waits for them, and re-layouts  2.5 us (4%)
    pallas_call x1, Pallas kernels, on_device(): pl.pallas_call(kernel, out_shape=(pltpu.VMEM((ROWS, SLOTS, BS, BS), BF16)...  67.1 us
    unnamed x2, local copies, waits for them, and re-layouts  2.5 us

profile of v5, /device:TPU:1, one launch (start us, length us, event | category | flops | bytes accessed | tf_op | source)
XLA Modules:
  0.0 70.2 jit_solution(9451553987843462104)
XLA Ops:
  0.6 67.1 %purify.1 = (bf16[8,15,128,128]{3,2,1,0:T(8,128)(2,1)S(1)}, f32[4,128]{1,0:T(4,128)S(1)}) custom-call(bf16[8,15,128,128]{3,2,1,0:T(8,128)(2,1)} %density.1, s32[8,15]{1,0:T(8,128)} %mask.1, s32[128]{0:T(128)} %slabs.1, s32[8,128]{1,0:T(8,128)} %bitcast.4, f32[3,512]{1,0:T(4,128)} %positions.1, f32[4,128]{1,0:T(4,128)} %bitcast.5), custom_call_target="tpu_custom_call" | custom-call | flops 10000000000 | bytes 10000000 | tf_op jit(solution)/shard_map/purify/pallas_call | solution.py:365
  67.7 1.9 %copy.10 = bf16[8,15,128,128]{3,2,1,0:T(8,128)(2,1)} copy(bf16[8,15,128,128]{3,2,1,0:T(8,128)(2,1)S(1)} %get-tuple-element.6) | data formatting | bytes 7864320
  69.6 0.6 copy.11

commit v6 on v5

--- a/solution.py
+++ b/solution.py
@@ -246,16 +246,24 @@
         left[i * BS:(i + 1) * BS, SPAN + i * BS:SPAN + (i + 1) * BS] = block
         right[SPAN + i * BS:SPAN + (i + 1) * BS, i * BS:(i + 1) * BS] = block
 
-    halo_pair(0)
-    corners(0)
-    for n in range(1, BAND):
+    for a in range(0, ROWS, 2):
+        own = slice(a * BS, (a + 2) * BS)
+        outer[own, own] = dot(left[own, SPAN:2 * SPAN], right[SPAN:2 * SPAN, own])
+    for n in range(BAND):
         halo_pair(n)
+        corners(n)
     start_pair(0)
 
     def middle(a, b):
         first, last = max(a, b) + 1, min(a, b) + 16
         window = slice(first * BS, (last + 1) * BS)
-        total = dot(left[a * BS:(a + 2) * BS, window], right[window, b * BS:(b + 2) * BS])
+        rows, columns = slice(a * BS, (a + 2) * BS), slice(b * BS, (b + 2) * BS)
+        if a == b:
+            total = outer[rows, columns]
+            for window in (slice(first * BS, SPAN), slice(2 * SPAN, (last + 1) * BS)):
+                total = total + dot(left[rows, window], right[window, columns])
+        else:
+            total = dot(left[rows, window], right[window, columns])
         for i in (a, a + 1):
             for j in (b, b + 1):
                 s = j - i + BAND
@@ -280,8 +288,6 @@
         )
         copy.start()
         rho_copies.append(copy)
-    for n in range(1, BAND):
-        corners(n)
     for copy in rho_copies:
         copy.wait()
     for n in range(1, BAND):

time: 71.3 us -> 72.7 us (1.020); the launches traced: 70.2 us -> 72.6 us
  Pallas kernels: 67.1 us -> 69.4 us
    pallas_call x1, Pallas kernels: 67.1 us -> 69.4 us  [on_device(): pl.pallas_call(kernel, out_shape=(pltpu.VMEM((ROWS, SLOTS, BS, BS), BF16)...]
where the time goes in v6:
time: 72.7 us; the launch traced here: 72.6 us
  Pallas kernels  69.4 us (95%)
  local copies, waits for them, and re-layouts  2.5 us (3%)
    pallas_call x1, Pallas kernels, on_device(): pl.pallas_call(kernel, out_shape=(pltpu.VMEM((ROWS, SLOTS, BS, BS), BF16)...  69.4 us
    unnamed x2, local copies, waits for them, and re-layouts  2.5 us

profile of v6, /device:TPU:1, one launch (start us, length us, event | category | flops | bytes accessed | tf_op | source)
XLA Modules:
  0.0 72.6 jit_solution(99494981553140973)
XLA Ops:
  0.6 69.4 %purify.1 = (bf16[8,15,128,128]{3,2,1,0:T(8,128)(2,1)S(1)}, f32[4,128]{1,0:T(4,128)S(1)}) custom-call(bf16[8,15,128,128]{3,2,1,0:T(8,128)(2,1)} %density.1, s32[8,15]{1,0:T(8,128)} %mask.1, s32[128]{0:T(128)} %slabs.1, s32[8,128]{1,0:T(8,128)} %bitcast.4, f32[3,512]{1,0:T(4,128)} %positions.1, f32[4,128]{1,0:T(4,128)} %bitcast.5), custom_call_target="tpu_custom_call" | custom-call | flops 10000000000 | bytes 10000000 | tf_op jit(solution)/shard_map/purify/pallas_call | solution.py:371
  70.1 1.9 %copy.10 = bf16[8,15,128,128]{3,2,1,0:T(8,128)(2,1)} copy(bf16[8,15,128,128]{3,2,1,0:T(8,128)(2,1)S(1)} %get-tuple-element.6) | data formatting | bytes 7864320
  72.0 0.6 copy.11
